TPU v7x, 32 devices: a whole 2x2x4 slice. The times are simulated.
32 devices in a mesh: dp: 4 (over x, core), space: 8 (over z, y).
Axes of the slice: x: 2, y: 2, z: 4, core: 2. Of those that a mesh axis runs over, the one named last changes fastest.
Arguments:
- acts_in: bfloat16 [4, 32, 64, 32, 128], P('dp', 'space'), may hold values from -6 to 6
- pre_act: bfloat16 [4, 32, 64, 32, 128], P('dp', 'space'), may hold values from -6 to 6
- weight_two: bfloat16 [128, 3, 3, 3, 128], P('space'), may hold values from -0.109375 to 0.109375
- grad_out: bfloat16 [4, 16, 32, 16, 128], P('dp', None, None, None, 'space'), may hold values from -6 to 6
Outputs:
- fine_grad: float32 [128, 3, 3, 3, 128], P('space')
- coarse_grad: float32 [128, 3, 3, 3, 128], P('space')
All inputs are finite; a program needn't handle non-finite values.
Results may differ from a plain program's by a relative error of at most 0.003.
Values may be sent and summed in bfloat16 or wider, within the bound.
A program may use at most 128 MiB of HBM per device.

v0:
```python
import functools
import math

import jax
import jax.numpy as jnp
from jax import lax
from jax.experimental import pallas as pl
from jax.experimental.pallas import tpu as pltpu
from jax.sharding import PartitionSpec as P

leak_slope = 0.3
parity_taps = {0: ((1, 0),), 1: ((0, 1), (2, 0))}
MESH = pl.DeviceIdType.MESH
VMEM = pltpu.VMEM
f32, bf16 = jnp.float32, jnp.bfloat16


def remote(src, dst, send, recv, target):
    return pltpu.make_async_remote_copy(
        src_ref=src,
        dst_ref=dst,
        send_sem=send,
        recv_sem=recv,
        device_id=target,
        device_id_type=MESH,
    )


def greet(dp, parts):
    me, mine = lax.axis_index("space"), lax.axis_index("dp")
    barrier = pltpu.get_barrier_semaphore()
    for d in range(1, parts):
        pl.semaphore_signal(
            barrier, inc=1, device_id={"space": lax.rem(me + d, parts)}, device_id_type=MESH
        )
    for d in range(1, dp):
        pl.semaphore_signal(
            barrier, inc=1, device_id={"dp": lax.rem(mine + d, dp)}, device_id_type=MESH
        )
    pl.semaphore_wait(barrier, parts + dp - 2)


class Reduction:
    def __init__(self, dp, parts, scaling, out, part, scratch):
        self.dp, self.parts, self.scaling, self.out, self.part = dp, parts, scaling, out, part
        self.got, self.away, self.came, self.apart, self.near, self.whole, self.sends, self.recvs = scratch
        self.me, self.mine = lax.axis_index("space"), lax.axis_index("dp")
        self.core = lax.rem(self.mine, 2)
        self.rest = self.mine // 2
        self.ranks = dp // 2
        self.chunk = part.shape[0] // dp
        self.half = self.chunk * self.ranks
        self.order = list(range(1, self.ranks)) + [0]
        self.rows = part.shape[1] // parts
        self.inputs = part.shape[2]

    def to_core(self):
        self.first = []
        theirs = (1 - self.core) * self.half
        for d in self.order:
            j = lax.rem(self.rest + d, self.ranks)
            copy = remote(
                self.part.at[pl.ds(theirs + j * self.chunk, self.chunk)],
                self.got.at[d],
                self.sends.at[0, d],
                self.recvs.at[0, d],
                {"dp": self.mine + 1 - 2 * self.core},
            )
            copy.start()
            self.first.append(copy)

    def to_chips(self):
        self.second = []
        for d, copy in zip(self.order, self.first):
            j = lax.rem(self.rest + d, self.ranks)
            base = self.core * self.half + j * self.chunk
            copy.wait_recv()
            if d:

                def fill(u, carry):
                    self.away[d - 1, u] = (self.part[base + u] + self.got[d, u]).astype(bf16)
                    return carry

                lax.fori_loop(0, self.chunk, fill, 0)
                onward = remote(
                    self.away.at[d - 1],
                    self.came.at[d - 1],
                    self.sends.at[1, d],
                    self.recvs.at[1, d],
                    {"dp": 2 * j + self.core},
                )
                onward.start()
                self.second.append(onward)

    def to_space(self):
        base = self.core * self.half + self.rest * self.chunk
        for onward in self.second:
            onward.wait_recv()

        def settle(u, carry):
            total = self.part[base + u] + self.got[0, u]
            for d in range(1, self.ranks):
                total = total + self.came[d - 1, u].astype(f32)
            self.got[0, u] = total
            return carry

        lax.fori_loop(0, self.chunk, settle, 0)
        self.third = []
        for d in range(1, self.parts):
            t = lax.rem(self.me + d, self.parts)
            self.apart[d - 1] = self.block(t).astype(bf16)
            copy = remote(
                self.apart.at[d - 1],
                self.near.at[d - 1],
                self.sends.at[2, d],
                self.recvs.at[2, d],
                {"space": t},
            )
            copy.start()
            self.third.append(copy)

    def block(self, t):
        start = pl.multiple_of(t * self.rows, self.rows)
        taps = self.got[0, :, pl.ds(start, self.rows), :]
        return taps.reshape(self.chunk * self.rows, self.inputs)

    def to_copies(self):
        total = self.block(self.me)
        for d in range(1, self.parts):
            self.third[d - 1].wait_recv()
            total = total + self.near[d - 1].astype(f32)
        self.whole[0] = total * self.scaling
        self.fourth = []
        for d in range(1, self.dp):
            copy = remote(
                self.whole.at[0],
                self.whole.at[d],
                self.sends.at[3, d],
                self.recvs.at[3, d],
                {"dp": lax.rem(self.mine + d, self.dp)},
            )
            copy.start()
            self.fourth.append(copy)

    def finish(self):
        self.out[self.core * self.ranks + self.rest] = self.whole[0]
        for d in range(1, self.dp):
            self.fourth[d - 1].wait_recv()
            other = lax.rem(self.mine + self.dp - d, self.dp)
            self.out[lax.rem(other, 2) * self.ranks + other // 2] = self.whole[d]
        for copy in self.first + self.second + self.third + self.fourth:
            copy.wait_send()


def kernel(dp, parts, scaling, sizes, acts, pre, w_ref, g_ref, coarse_out, fine_out, *scratch):
    coarse_sum = Reduction(dp, parts, scaling, coarse_out, scratch[0], scratch[1:9])
    fine_sum = Reduction(dp, parts, scaling, fine_out, scratch[9], scratch[10:18])
    (wbuf, gbuf, halo, sends, recvs, w_full, mixing, g_turned, g_rows, values, thin, frame, delta) = scratch[18:]
    coarse, fine = scratch[0], scratch[9]
    depth, across, height, channels = sizes
    half_x, half_y, half_z = depth // 2, across // 2, height // 2
    plane, small = across * height, half_y * half_z
    rows = channels // parts
    me, mine = lax.axis_index("space"), lax.axis_index("dp")
    core = lax.rem(mine, 2)
    partner = mine + 1 - 2 * core
    half = w_ref.shape[0] // 2
    greet(dp, parts)

    g_copies, w_copies, forwards = [], [], []
    for d in range(1, parts):
        t = lax.rem(me + d, parts)
        copy = remote(g_ref.at[t], gbuf.at[d - 1], sends.at[0, d], recvs.at[0, d], {"space": t})
        copy.start()
        g_copies.append(copy)
    own = w_ref.at[pl.ds(pl.multiple_of(core * half, 16), half)]
    for d in range(1, parts):
        t = lax.rem(me + d, parts)
        copy = remote(own, wbuf.at[d - 1, core], sends.at[1, d], recvs.at[1, d], {"space": t})
        copy.start()
        w_copies.append(copy)
    upward = remote(
        acts.at[depth - 1],
        halo.at[0],
        sends.at[2, 0],
        recvs.at[2, 0],
        {"space": lax.rem(me + 1, parts)},
    )
    downward = remote(
        acts.at[0],
        halo.at[1],
        sends.at[0, 0],
        recvs.at[0, 0],
        {"space": lax.rem(me + parts - 1, parts)},
    )
    pl.when(me < parts - 1)(upward.start)
    pl.when(me > 0)(downward.start)

    at_z = lax.broadcasted_iota(jnp.int32, (small, channels), 0) % half_z

    def spread(x, carry):
        values[x] = pre[x].astype(f32).reshape(half_y, 2, height, channels)
        for odd_y in (0, 1):
            pair = []
            for odd_z in (0, 1):
                cells = values[x, :, odd_y, pl.ds(odd_z, half_z, stride=2), :]
                cells = cells.reshape(small, channels)
                pair.append(jnp.where(cells > 0, cells, leak_slope * cells))
            earlier = jnp.where(at_z == 0, 0.0, pltpu.roll(pair[1], 1, 0))
            row = half_z * odd_y
            thin[x, odd_y, pl.ds(row, small), 0:channels] = earlier.astype(bf16)
            thin[x, odd_y, pl.ds(row, small), channels : 2 * channels] = pair[0].astype(bf16)
            thin[x, odd_y, pl.ds(row, small), 2 * channels :] = pair[1].astype(bf16)
        thin[x, 1, 0:half_z, :] = jnp.zeros((half_z, 3 * channels), bf16)
        return carry

    lax.fori_loop(0, depth, spread, 0)

    at_cell = lax.broadcasted_iota(jnp.int32, (plane, channels), 0) % height

    def place(q, cells):
        cells = cells.astype(f32)
        inner = pl.ds(height, plane)
        earlier = jnp.where(at_cell == 0, 0.0, pltpu.roll(cells, 1, 0))
        later = jnp.where(at_cell == height - 1, 0.0, pltpu.roll(cells, plane - 1, 0))
        frame[q, inner, 0:channels] = earlier.astype(bf16)
        frame[q, inner, channels : 2 * channels] = cells.astype(bf16)
        frame[q, inner, 2 * channels :] = later.astype(bf16)
        nothing = jnp.zeros((height, 3 * channels), bf16)
        frame[q, 0:height, :] = nothing
        frame[q, pl.ds(height + plane, height), :] = nothing

    def place_own(x, carry):
        place(x + 1, acts[x])
        return carry

    lax.fori_loop(0, depth, place_own, 0)

    def take_filters(s, part, block):
        block = block.astype(f32).reshape(half // rows, rows, channels)
        start = pl.multiple_of(s * rows, rows)
        w_full[pl.ds(part * (half // rows), half // rows), pl.ds(start, rows), :] = block

    def take_cotangents(s, block):
        g_turned[pl.ds(pl.multiple_of(s * rows, rows), rows), :] = block.astype(f32)

    take_cotangents(me, g_ref[me])
    for part in (0, 1):
        take_filters(me, part, w_ref[part * half : (part + 1) * half])
    for d in range(1, parts):
        g_copies[d - 1].wait_recv()
        take_cotangents(lax.rem(me + parts - d, parts), gbuf[d - 1])
    for d in range(1, parts):
        w_copies[d - 1].wait_recv()
        block = wbuf.at[d - 1, core]
        copy = remote(block, block, sends.at[2, d], recvs.at[2, d], {"dp": partner})
        copy.start()
        forwards.append(copy)

    for tap_x in range(3):
        for tap_y in range(3):
            total = None
            for p in range(half_x):
                at_p, at_x = (p + 1, 2 * p + 1) if tap_x == 0 else (p, 2 * p + tap_x - 1)
                lhs = g_turned[:, at_p * small : (at_p + 1) * small].astype(bf16)
                row = half_z if tap_y == 2 else 0
                rhs = thin[at_x, 0 if tap_y == 1 else 1, row : row + small, :]
                term = jnp.dot(lhs, rhs, preferred_element_type=f32)
                total = term if total is None else total + term
            for tap_z in range(3):
                coarse[9 * tap_x + 3 * tap_y + tap_z] = total[
                    :, tap_z * channels : (tap_z + 1) * channels
                ]
    for u in range(27, coarse.shape[0]):
        coarse[u] = jnp.zeros((channels, channels), f32)
    coarse_sum.to_core()

    for p in range(half_x + 1):
        cells = g_turned[:, p * small : (p + 1) * small].T
        later = jnp.where(at_z == half_z - 1, 0.0, pltpu.roll(cells, small - 1, 0))
        g_rows[p, 0:small, 0:channels] = cells.astype(bf16)
        g_rows[p, 0:small, channels:] = later.astype(bf16)
        g_rows[p, small : small + half_z, :] = jnp.zeros((half_z, 2 * channels), bf16)

    for d in range(1, parts):
        forwards[d - 1].wait_recv()
        s = lax.rem(me + parts - d, parts)
        for part in (0, 1):
            take_filters(s, part, wbuf[d - 1, part])

    def mix(t, carry):
        mixing[t, 0:channels, 0:channels] = w_full[3 * t + 1].astype(bf16)
        mixing[t, 0:channels, channels:] = w_full[3 * t + 2].astype(bf16)
        mixing[t, channels:, 0:channels] = jnp.zeros((channels, channels), bf16)
        mixing[t, channels:, channels:] = w_full[3 * t].astype(bf16)
        return carry

    lax.fori_loop(0, 9, mix, 0)
    coarse_sum.to_chips()

    def propagate(p, carry):
        for odd_x in (0, 1):
            for odd_y in (0, 1):
                total = None
                for tap_x, move_x in parity_taps[odd_x]:
                    for tap_y, move_y in parity_taps[odd_y]:
                        cells = g_rows[p + move_x, move_y * half_z : move_y * half_z + small, :]
                        term = jnp.dot(
                            cells, mixing[3 * tap_x + tap_y], preferred_element_type=f32
                        )
                        total = term if total is None else total + term
                for odd_z in (0, 1):
                    where = (2 * p + odd_x, slice(None), odd_y, pl.ds(odd_z, half_z, stride=2))
                    before = values[where].reshape(small, channels)
                    piece = total[:, odd_z * channels : (odd_z + 1) * channels]
                    piece = piece * jnp.where(before > 0, 1.0, leak_slope)
                    values[where] = piece.reshape(half_y, half_z, channels)
        for odd_x in (0, 1):
            x = 2 * p + odd_x
            cells = values[x].reshape(plane, channels)
            delta[pl.ds(pl.multiple_of(x * channels, channels), channels), :] = cells.T.astype(bf16)
        return carry

    lax.fori_loop(0, half_x, propagate, 0)

    def clear(u, carry):
        fine[u] = jnp.zeros((channels, channels), f32)
        return carry

    lax.fori_loop(0, fine.shape[0], clear, 0)

    def layer(q):
        low, high = max(0, q - 2), min(depth - 1, q)

        def step(tap_y, carry):
            rhs = frame[q, pl.ds(pl.multiple_of(tap_y * height, height), plane), :]
            lhs = delta[low * channels : (high + 1) * channels, :]
            total = jnp.dot(lhs, rhs, preferred_element_type=f32)
            for x in range(low, high + 1):
                for tap_z in range(3):
                    fine[9 * (q - x) + 3 * tap_y + tap_z] += total[
                        (x - low) * channels : (x - low + 1) * channels,
                        tap_z * channels : (tap_z + 1) * channels,
                    ]
            return carry

        lax.fori_loop(0, 3, step, 0)

    layer(1)
    coarse_sum.to_space()
    for q in range(2, depth):
        layer(q)
    coarse_sum.to_copies()
    layer(depth)

    @pl.when(me > 0)
    def _():
        upward.wait_recv()
        place(0, halo[0])
        layer(0)

    @pl.when(me < parts - 1)
    def _():
        downward.wait_recv()
        place(depth + 1, halo[1])
        layer(depth + 1)

    fine_sum.to_core()
    coarse_sum.finish()
    fine_sum.to_chips()
    fine_sum.to_space()
    fine_sum.to_copies()
    fine_sum.finish()
    for copy in g_copies + w_copies + forwards:
        copy.wait_send()
    pl.when(me < parts - 1)(upward.wait_send)
    pl.when(me > 0)(downward.wait_send)


def reduction_scratch(dp, parts, channels):
    chunk = -(-27 // dp)
    ranks = dp // 2
    rows = channels // parts
    most = max(dp, parts)
    return [
        VMEM((chunk * dp, channels, channels), f32),
        VMEM((ranks, chunk, channels, channels), f32),
        VMEM((ranks - 1, chunk, channels, channels), bf16),
        VMEM((ranks - 1, chunk, channels, channels), bf16),
        VMEM((parts - 1, chunk * rows, channels), bf16),
        VMEM((parts - 1, chunk * rows, channels), bf16),
        VMEM((dp, chunk * rows, channels), f32),
        pltpu.SemaphoreType.DMA((4, most)),
        pltpu.SemaphoreType.DMA((4, most)),
    ]


def gradients(dp, parts, scaling, sizes, acts, pre, w, g):
    depth, across, height, channels = sizes
    half_x, half_y, half_z = depth // 2, across // 2, height // 2
    plane, small = across * height, half_y * half_z
    chunk = -(-27 // dp)
    rows = channels // parts
    half = w.shape[0] // 2
    flops = 2 * 27 * channels * channels * (depth * plane + 2 * half_x * small)
    return pl.pallas_call(
        functools.partial(kernel, dp, parts, scaling, sizes),
        out_shape=[jax.ShapeDtypeStruct((dp, chunk * rows, channels), f32)] * 2,
        in_specs=[pl.BlockSpec(memory_space=VMEM)] * 4,
        out_specs=[pl.BlockSpec(memory_space=VMEM)] * 2,
        scratch_shapes=reduction_scratch(dp, parts, channels)
        + reduction_scratch(dp, parts, channels)
        + [
            VMEM((parts - 1, 2, half, channels), bf16),
            VMEM((parts - 1,) + g.shape[1:], bf16),
            VMEM((2, plane, channels), bf16),
            pltpu.SemaphoreType.DMA((3, parts)),
            pltpu.SemaphoreType.DMA((3, parts)),
            VMEM((28, channels, channels), f32),
            VMEM((9, 2 * channels, 2 * channels), bf16),
            VMEM((channels, (half_x + 1) * small), f32),
            VMEM((half_x + 1, small + half_z, 2 * channels), bf16),
            VMEM((depth, half_y, 2, height, channels), f32),
            VMEM((depth, 2, small + half_z, 3 * channels), bf16),
            VMEM((depth + 2, plane + 2 * height, 3 * channels), bf16),
            VMEM((depth * channels, plane), bf16),
        ],
        cost_estimate=pl.CostEstimate(flops=flops, bytes_accessed=8 << 20, transcendentals=0),
        compiler_params=pltpu.CompilerParams(
            collective_id=0, has_side_effects=True, vmem_limit_bytes=56 << 20
        ),
    )(acts, pre, w, g)


def body(acts_in, pre_act, weight_two, grad_out):
    parts = lax.axis_size("space")
    groups = lax.axis_size("dp")
    depth, across, height, channels = sizes = acts_in.shape[1:]
    rows = weight_two.shape[0]
    scaling = 1.0 / math.sqrt(groups * depth * parts * across * height)
    small = across * height // 4
    turned = grad_out[0].reshape(parts, depth // 2 * small, rows).transpose(0, 2, 1)
    following = jnp.pad(turned[1:, :, :small], ((0, 1), (0, 0), (0, 0)))
    pieces = jnp.concatenate([turned, following], axis=2)
    shard = weight_two.reshape(rows, 27, channels).transpose(1, 0, 2)
    shard = jnp.pad(shard, ((0, 1), (0, 0), (0, 0))).reshape(28 * rows, channels)
    flat = (depth, across * height, channels)
    coarse, fine = gradients(
        groups, parts, scaling, sizes, acts_in.reshape(flat), pre_act.reshape(flat), shard, pieces
    )

    def by_filter(totals):
        taps = totals.reshape(-1, rows, channels)[:27]
        return taps.transpose(1, 0, 2).reshape(rows, 3, 3, 3, channels)

    return (by_filter(fine), by_filter(coarse))


def solution(mesh):
    placed = (
        P("dp", "space", None, None, None),
        P("dp", "space", None, None, None),
        P("space", None, None, None, None),
        P("dp", None, None, None, "space"),
    )
    return jax.shard_map(
        body,
        mesh=mesh,
        in_specs=placed,
        out_specs=(P("space", None, None, None, None), P("space", None, None, None, None)),
        check_vma=False,
    )
```

profile of v0, /device:TPU:0, one launch (start us, length us, event | category | flops | bytes accessed | tf_op | source)
XLA Modules:
  0.0 81.5 jit_solution(15615381229062197785)
XLA Ops:
  0.6 2.1 %copy.6 = bf16[1,16,32,16,16]{3,2,1,4,0:T(8,128)(2,1)S(1)} copy(bf16[1,16,32,16,16]{2,4,3,1,0:T(8,128)(2,1)} %param.7) | data formatting | bytes 524288 | tf_op args[3]
  2.7 0.0 copy-start
  2.7 3.6 %reshape_squeeze.3 = bf16[8,1024,16]{1,0,2:T(8,128)(2,1)S(1)} reshape(bf16[1,16,32,16,16]{3,2,1,4,0:T(8,128)(2,1)S(1)} %copy.6) | data formatting | bytes 524288 | tf_op jit(solution)/shard_map/reshape;squeeze | solution.py:442
  6.3 0.2 copy.9
  6.5 0.8 fusion.1.g_ref
  7.3 0.0 copy-done
  7.3 0.7 pad.8
  7.9 70.3 %shard_map.59 = (f32[4,112,128]{2,1,0:T(8,128)}, f32[4,112,128]{2,1,0:T(8,128)}) custom-call(bf16[4,2048,128]{2,1,0:T(8,128)(2,1)} %bitcast.29, bf16[4,2048,128]{2,1,0:T(8,128)(2,1)} %bitcast.30, bf16[448,128]{1,0:T(8,128)(2,1)} %bitcast.27, bf16[8,16,1536]{2,1,0:T(8,128)(2,1)} %fusion.1.g_ref), custom_call_target="tpu_custom_call" | custom-call | flops 9059696640 | bytes 8388608 | tf_op jit(solution)/shard_map/pallas_call | solution.py:406
  78.2 1.6 %slice.14 = f32[27,16,128]{2,1,0:T(8,128)} slice(f32[28,16,128]{2,1,0:T(8,128)} %bitcast.26), slice={[0:27], [0:16], [0:128]} | slice | bytes 442368 | tf_op jit(solution)/shard_map/slice | solution.py:453
  79.9 1.6 %slice.13 = f32[27,16,128]{2,1,0:T(8,128)} slice(f32[28,16,128]{2,1,0:T(8,128)} %bitcast.25), slice={[0:27], [0:16], [0:128]} | slice | bytes 442368 | tf_op jit(solution)/shard_map/slice | solution.py:453
  (1 shorter events, 0.0 us)
Async XLA Ops:
  2.7 4.6 %copy-start = (bf16[16,3,3,3,128]{4,0,3,2,1:T(8,128)(2,1)S(1)}, bf16[16,3,3,3,128]{4,0,3,2,1:T(8,128)(2,1)}, u32[]{:S(2)}) copy-start(bf16[16,3,3,3,128]{4,0,3,2,1:T(8,128)(2,1)} %param.6) | copy-start | bytes 331780
where the time goes:
time: 81.7 us; the launch traced here: 81.5 us
  Pallas kernels  70.3 us (86%)
  local copies, waits for them, and re-layouts  9.75 us (12%)
    pallas_call x1, Pallas kernels, gradients(): pl.pallas_call(functools.partial(kernel, dp, parts, scaling, sizes), out_...  70.3 us
    another operation x2, local copies, waits for them, and re-layouts, body(): grad_out[0].reshape(parts, depth // 2 * small, rows).transpose(0, 2, 1)  3.73 us
    slice x2, local copies, waits for them, and re-layouts, by_filter(): taps = totals.reshape(-1, rows, channels)[:27]  3.27 us
    unnamed x3, local copies, waits for them, and re-layouts  2.09 us

commit v1 on v0

--- a/solution.py
+++ b/solution.py
@@ -26,7 +26,7 @@
     )
 
 
-def greet(dp, parts):
+def hello(dp, parts):
     me, mine = lax.axis_index("space"), lax.axis_index("dp")
     barrier = pltpu.get_barrier_semaphore()
     for d in range(1, parts):
@@ -37,11 +37,11 @@
         pl.semaphore_signal(
             barrier, inc=1, device_id={"dp": lax.rem(mine + d, dp)}, device_id_type=MESH
         )
-    pl.semaphore_wait(barrier, parts + dp - 2)
 
 
 class Reduction:
-    def __init__(self, dp, parts, scaling, out, part, scratch):
+    def __init__(self, dp, parts, scaling, out, place, part, scratch):
+        self.place = place
         self.dp, self.parts, self.scaling, self.out, self.part = dp, parts, scaling, out, part
         self.got, self.away, self.came, self.apart, self.near, self.whole, self.sends, self.recvs = scratch
         self.me, self.mine = lax.axis_index("space"), lax.axis_index("dp")
@@ -142,21 +142,36 @@
             copy.start()
             self.fourth.append(copy)
 
+    def put(self, c, d):
+        for u in range(self.chunk):
+            taps = self.whole[d, u * self.rows : (u + 1) * self.rows, :]
+            self.out[self.place(c * self.chunk + u)] = taps
+
     def finish(self):
-        self.out[self.core * self.ranks + self.rest] = self.whole[0]
+        self.put(self.core * self.ranks + self.rest, 0)
         for d in range(1, self.dp):
             self.fourth[d - 1].wait_recv()
             other = lax.rem(self.mine + self.dp - d, self.dp)
-            self.out[lax.rem(other, 2) * self.ranks + other // 2] = self.whole[d]
+            self.put(lax.rem(other, 2) * self.ranks + other // 2, d)
         for copy in self.first + self.second + self.third + self.fourth:
             copy.wait_send()
 
 
+def middle_place(u):
+    return u + 9 + 18 * (u // 9)
+
+
+def outer_place(u):
+    return u + 9 * (u // 9)
+
+
 def kernel(dp, parts, scaling, sizes, acts, pre, w_ref, g_ref, coarse_out, fine_out, *scratch):
-    coarse_sum = Reduction(dp, parts, scaling, coarse_out, scratch[0], scratch[1:9])
-    fine_sum = Reduction(dp, parts, scaling, fine_out, scratch[9], scratch[10:18])
-    (wbuf, gbuf, halo, sends, recvs, w_full, mixing, g_turned, g_rows, values, thin, frame, delta) = scratch[18:]
-    coarse, fine = scratch[0], scratch[9]
+    coarse, middle, outer = scratch[0], scratch[9], scratch[18]
+    share = (dp, parts, scaling)
+    coarse_sum = Reduction(*share, coarse_out, lambda u: u, coarse, scratch[1:9])
+    middle_sum = Reduction(*share, fine_out, middle_place, middle, scratch[10:18])
+    outer_sum = Reduction(*share, fine_out, outer_place, outer, scratch[19:27])
+    (wbuf, gbuf, halo, sends, recvs, w_full, mixing, g_send, g_turned, g_mixed, g_cells, g_rows, values, thin, frame, delta) = scratch[27:]
     depth, across, height, channels = sizes
     half_x, half_y, half_z = depth // 2, across // 2, height // 2
     plane, small = across * height, half_y * half_z
@@ -164,37 +179,52 @@
     me, mine = lax.axis_index("space"), lax.axis_index("dp")
     core = lax.rem(mine, 2)
     partner = mine + 1 - 2 * core
-    half = w_ref.shape[0] // 2
-    greet(dp, parts)
-
-    g_copies, w_copies, forwards = [], [], []
+    half = (w_ref.shape[0] + 1) // 2
+    beside = me + 1 - 2 * lax.rem(me, 2)
+    hello(dp, parts)
+
+    count = 128 // half_y
+
+    def pack(x, carry):
+        for group in range(half_z // count):
+            cells = [g_ref[x, group * count + j].astype(f32) for j in range(count)]
+            g_send[x, :, group * 128 : (group + 1) * 128] = jnp.concatenate(cells, axis=1).astype(bf16)
+        return carry
+
+    lax.fori_loop(0, g_ref.shape[0], pack, 0)
+    g_send[g_ref.shape[0]] = jnp.zeros((rows, small), bf16)
+    pl.semaphore_wait(pltpu.get_barrier_semaphore(), parts + dp - 2)
+
+    g_copies, w_copies, w_beside, forwards = [], [], [], []
     for d in range(1, parts):
         t = lax.rem(me + d, parts)
-        copy = remote(g_ref.at[t], gbuf.at[d - 1], sends.at[0, d], recvs.at[0, d], {"space": t})
+        mine_there = g_send.at[pl.ds(t * half_x, half_x + 1)]
+        copy = remote(mine_there, gbuf.at[d - 1], sends.at[0, d], recvs.at[0, d], {"space": t})
         copy.start()
         g_copies.append(copy)
-    own = w_ref.at[pl.ds(pl.multiple_of(core * half, 16), half)]
-    for d in range(1, parts):
-        t = lax.rem(me + d, parts)
-        copy = remote(own, wbuf.at[d - 1, core], sends.at[1, d], recvs.at[1, d], {"space": t})
+    own = w_ref.at[pl.ds(core * (half - 1), half)]
+    for i in range(1, parts // 2):
+        t = lax.rem(me + 2 * i, parts)
+        copy = remote(own, wbuf.at[0, i, core], sends.at[1, i], recvs.at[1, i], {"space": t})
         copy.start()
         w_copies.append(copy)
+    copy = remote(own, wbuf.at[1, 0, core], sends.at[2, 0], recvs.at[2, 0], {"space": beside})
+    copy.start()
+    w_beside.append(copy)
     upward = remote(
         acts.at[depth - 1],
         halo.at[0],
-        sends.at[2, 0],
-        recvs.at[2, 0],
+        sends.at[5, 0],
+        recvs.at[5, 0],
         {"space": lax.rem(me + 1, parts)},
     )
     downward = remote(
         acts.at[0],
         halo.at[1],
-        sends.at[0, 0],
-        recvs.at[0, 0],
+        sends.at[5, 1],
+        recvs.at[5, 1],
         {"space": lax.rem(me + parts - 1, parts)},
     )
-    pl.when(me < parts - 1)(upward.start)
-    pl.when(me > 0)(downward.start)
 
     at_z = lax.broadcasted_iota(jnp.int32, (small, channels), 0) % half_z
 
@@ -236,33 +266,39 @@
 
     lax.fori_loop(0, depth, place_own, 0)
 
-    def take_filters(s, part, block):
-        block = block.astype(f32).reshape(half // rows, rows, channels)
+    def take_cotangents(s, block):
         start = pl.multiple_of(s * rows, rows)
-        w_full[pl.ds(part * (half // rows), half // rows), pl.ds(start, rows), :] = block
-
-    def take_cotangents(s, block):
-        g_turned[pl.ds(pl.multiple_of(s * rows, rows), rows), :] = block.astype(f32)
-
-    take_cotangents(me, g_ref[me])
-    for part in (0, 1):
-        take_filters(me, part, w_ref[part * half : (part + 1) * half])
+        g_turned[:, pl.ds(start, rows), :] = block.astype(f32)
+
+    take_cotangents(me, g_send[pl.ds(me * half_x, half_x + 1)])
     for d in range(1, parts):
         g_copies[d - 1].wait_recv()
         take_cotangents(lax.rem(me + parts - d, parts), gbuf[d - 1])
-    for d in range(1, parts):
-        w_copies[d - 1].wait_recv()
-        block = wbuf.at[d - 1, core]
-        copy = remote(block, block, sends.at[2, d], recvs.at[2, d], {"dp": partner})
+    for p in range(half_x + 1):
+        g_mixed[p] = g_turned[p].T
+        for y in range(half_y):
+            cells = g_mixed[p, pl.ds(y, half_z, stride=half_y), :]
+            g_cells[p, y * half_z : (y + 1) * half_z, :] = cells
+        g_turned[p] = g_cells[p].T
+
+    for i in range(1, parts // 2):
+        w_copies[i - 1].wait_recv()
+        block = wbuf.at[0, i, core]
+        copy = remote(block, wbuf.at[1, i, core], sends.at[2, i], recvs.at[2, i], {"space": beside})
         copy.start()
-        forwards.append(copy)
+        w_beside.append(copy)
+        copy = remote(block, block, sends.at[3, i], recvs.at[3, i], {"dp": partner})
+        copy.start()
+        forwards.append((0, i, copy))
+    pl.when(me < parts - 1)(upward.start)
+    pl.when(me > 0)(downward.start)
 
     for tap_x in range(3):
         for tap_y in range(3):
             total = None
             for p in range(half_x):
                 at_p, at_x = (p + 1, 2 * p + 1) if tap_x == 0 else (p, 2 * p + tap_x - 1)
-                lhs = g_turned[:, at_p * small : (at_p + 1) * small].astype(bf16)
+                lhs = g_turned[at_p].astype(bf16)
                 row = half_z if tap_y == 2 else 0
                 rhs = thin[at_x, 0 if tap_y == 1 else 1, row : row + small, :]
                 term = jnp.dot(lhs, rhs, preferred_element_type=f32)
@@ -274,19 +310,31 @@
     for u in range(27, coarse.shape[0]):
         coarse[u] = jnp.zeros((channels, channels), f32)
     coarse_sum.to_core()
+    for i in range(parts // 2):
+        w_beside[i].wait_recv()
+        block = wbuf.at[1, i, core]
+        copy = remote(block, block, sends.at[4, i], recvs.at[4, i], {"dp": partner})
+        copy.start()
+        forwards.append((1, i, copy))
 
     for p in range(half_x + 1):
-        cells = g_turned[:, p * small : (p + 1) * small].T
+        cells = g_cells[p]
         later = jnp.where(at_z == half_z - 1, 0.0, pltpu.roll(cells, small - 1, 0))
         g_rows[p, 0:small, 0:channels] = cells.astype(bf16)
         g_rows[p, 0:small, channels:] = later.astype(bf16)
         g_rows[p, small : small + half_z, :] = jnp.zeros((half_z, 2 * channels), bf16)
 
-    for d in range(1, parts):
-        forwards[d - 1].wait_recv()
-        s = lax.rem(me + parts - d, parts)
+    def take_filters(s, part, block):
+        start = pl.multiple_of(s * rows, rows)
+        w_full[pl.ds(part * (half - 1), half), pl.ds(start, rows), :] = block.astype(f32)
+
+    for part in (0, 1):
+        take_filters(me, part, w_ref[part * (half - 1) : part * (half - 1) + half])
+    for side, i, copy in forwards:
+        copy.wait_recv()
+        source = beside if side else me
         for part in (0, 1):
-            take_filters(s, part, wbuf[d - 1, part])
+            take_filters(lax.rem(source + parts - 2 * i, parts), part, wbuf[side, i, part])
 
     def mix(t, carry):
         mixing[t, 0:channels, 0:channels] = w_full[3 * t + 1].astype(bf16)
@@ -324,10 +372,12 @@
     lax.fori_loop(0, half_x, propagate, 0)
 
     def clear(u, carry):
-        fine[u] = jnp.zeros((channels, channels), f32)
+        outer[u] = jnp.zeros((channels, channels), f32)
         return carry
 
-    lax.fori_loop(0, fine.shape[0], clear, 0)
+    lax.fori_loop(0, outer.shape[0], clear, 0)
+    for u in range(middle.shape[0]):
+        middle[u] = jnp.zeros((channels, channels), f32)
 
     def layer(q):
         low, high = max(0, q - 2), min(depth - 1, q)
@@ -337,8 +387,9 @@
             lhs = delta[low * channels : (high + 1) * channels, :]
             total = jnp.dot(lhs, rhs, preferred_element_type=f32)
             for x in range(low, high + 1):
+                into, first = (middle, 0) if q - x == 1 else (outer, 9 * ((q - x) // 2))
                 for tap_z in range(3):
-                    fine[9 * (q - x) + 3 * tap_y + tap_z] += total[
+                    into[first + 3 * tap_y + tap_z] += total[
                         (x - low) * channels : (x - low + 1) * channels,
                         tap_z * channels : (tap_z + 1) * channels,
                     ]
@@ -353,32 +404,39 @@
     coarse_sum.to_copies()
     layer(depth)
 
+    middle_sum.to_core()
+
     @pl.when(me > 0)
     def _():
         upward.wait_recv()
         place(0, halo[0])
         layer(0)
 
+    middle_sum.to_chips()
+
     @pl.when(me < parts - 1)
     def _():
         downward.wait_recv()
         place(depth + 1, halo[1])
         layer(depth + 1)
 
-    fine_sum.to_core()
+    outer_sum.to_core()
+    middle_sum.to_space()
+    outer_sum.to_chips()
     coarse_sum.finish()
-    fine_sum.to_chips()
-    fine_sum.to_space()
-    fine_sum.to_copies()
-    fine_sum.finish()
-    for copy in g_copies + w_copies + forwards:
+    middle_sum.to_copies()
+    outer_sum.to_space()
+    middle_sum.finish()
+    outer_sum.to_copies()
+    outer_sum.finish()
+    for copy in g_copies + w_copies + w_beside + [copy for _, _, copy in forwards]:
         copy.wait_send()
     pl.when(me < parts - 1)(upward.wait_send)
     pl.when(me > 0)(downward.wait_send)
 
 
-def reduction_scratch(dp, parts, channels):
-    chunk = -(-27 // dp)
+def reduction_scratch(dp, parts, channels, taps):
+    chunk = -(-taps // dp)
     ranks = dp // 2
     rows = channels // parts
     most = max(dp, parts)
@@ -401,24 +459,33 @@
     plane, small = across * height, half_y * half_z
     chunk = -(-27 // dp)
     rows = channels // parts
-    half = w.shape[0] // 2
+    half = (w.shape[0] + 1) // 2
+    units = [chunk * dp]
+    for taps, where in ((9, middle_place), (18, outer_place)):
+        units.append(where(-(-taps // dp) * dp - 1) + 1)
     flops = 2 * 27 * channels * channels * (depth * plane + 2 * half_x * small)
     return pl.pallas_call(
         functools.partial(kernel, dp, parts, scaling, sizes),
-        out_shape=[jax.ShapeDtypeStruct((dp, chunk * rows, channels), f32)] * 2,
+        out_shape=[
+            jax.ShapeDtypeStruct((n, rows, channels), f32) for n in (units[0], max(units[1:]))
+        ],
         in_specs=[pl.BlockSpec(memory_space=VMEM)] * 4,
         out_specs=[pl.BlockSpec(memory_space=VMEM)] * 2,
-        scratch_shapes=reduction_scratch(dp, parts, channels)
-        + reduction_scratch(dp, parts, channels)
+        scratch_shapes=reduction_scratch(dp, parts, channels, 27)
+        + reduction_scratch(dp, parts, channels, 9)
+        + reduction_scratch(dp, parts, channels, 18)
         + [
-            VMEM((parts - 1, 2, half, channels), bf16),
-            VMEM((parts - 1,) + g.shape[1:], bf16),
+            VMEM((2, parts // 2, 2, half, rows, channels), bf16),
+            VMEM((parts - 1, half_x + 1, rows, small), bf16),
             VMEM((2, plane, channels), bf16),
-            pltpu.SemaphoreType.DMA((3, parts)),
-            pltpu.SemaphoreType.DMA((3, parts)),
-            VMEM((28, channels, channels), f32),
+            pltpu.SemaphoreType.DMA((6, parts)),
+            pltpu.SemaphoreType.DMA((6, parts)),
+            VMEM((27, channels, channels), f32),
             VMEM((9, 2 * channels, 2 * channels), bf16),
-            VMEM((channels, (half_x + 1) * small), f32),
+            VMEM((g.shape[0] + 1, rows, small), bf16),
+            VMEM((half_x + 1, channels, small), f32),
+            VMEM((half_x + 1, small, channels), f32),
+            VMEM((half_x + 1, small, channels), f32),
             VMEM((half_x + 1, small + half_z, 2 * channels), bf16),
             VMEM((depth, half_y, 2, height, channels), f32),
             VMEM((depth, 2, small + half_z, 3 * channels), bf16),
@@ -438,19 +505,15 @@
     depth, across, height, channels = sizes = acts_in.shape[1:]
     rows = weight_two.shape[0]
     scaling = 1.0 / math.sqrt(groups * depth * parts * across * height)
-    small = across * height // 4
-    turned = grad_out[0].reshape(parts, depth // 2 * small, rows).transpose(0, 2, 1)
-    following = jnp.pad(turned[1:, :, :small], ((0, 1), (0, 0), (0, 0)))
-    pieces = jnp.concatenate([turned, following], axis=2)
+    turned = grad_out[0].transpose(0, 2, 3, 1)
     shard = weight_two.reshape(rows, 27, channels).transpose(1, 0, 2)
-    shard = jnp.pad(shard, ((0, 1), (0, 0), (0, 0))).reshape(28 * rows, channels)
     flat = (depth, across * height, channels)
     coarse, fine = gradients(
-        groups, parts, scaling, sizes, acts_in.reshape(flat), pre_act.reshape(flat), shard, pieces
+        groups, parts, scaling, sizes, acts_in.reshape(flat), pre_act.reshape(flat), shard, turned
     )
 
     def by_filter(totals):
-        taps = totals.reshape(-1, rows, channels)[:27]
+        taps = totals[:27]
         return taps.transpose(1, 0, 2).reshape(rows, 3, 3, 3, channels)
 
     return (by_filter(fine), by_filter(coarse))

time: 81.7 us -> 81.9 us (level)
  Pallas kernels: 70.3 us -> 77.8 us
  local copies, waits for them, and re-layouts: 9.75 us -> 3.27 us
    pallas_call x1, Pallas kernels: 70.3 us -> 77.8 us  [gradients(): pl.pallas_call(functools.partial(kernel, dp, parts, scaling, sizes), out_...]
    another operation x2 -> x0, local copies, waits for them, and re-layouts: 3.73 us -> none  [body(): grad_out[0].reshape(parts, depth // 2 * small, rows).transpose(0, 2, 1)]
    unnamed x3 -> x0, local copies, waits for them, and re-layouts: 2.09 us -> none
    slice x3 -> x2, local copies, waits for them, and re-layouts: 3.28 us -> 3.27 us  [by_filter(): taps = totals[:27]]
where the time goes in v1:
time: 81.9 us; the launch traced here: 81.8 us
  Pallas kernels  77.8 us (95%)
  local copies, waits for them, and re-layouts  3.27 us (4%)
    pallas_call x1, Pallas kernels, gradients(): pl.pallas_call(functools.partial(kernel, dp, parts, scaling, sizes), out_...  77.8 us
    slice x2, local copies, waits for them, and re-layouts, by_filter(): taps = totals[:27]  3.27 us

profile of v1, /device:TPU:0, one launch (start us, length us, event | category | flops | bytes accessed | tf_op | source)
XLA Modules:
  0.0 81.8 jit_solution(10440188047220103011)
XLA Ops:
  0.6 77.8 %shard_map.59 = (f32[28,16,128]{2,1,0:T(8,128)}, f32[39,16,128]{2,1,0:T(8,128)}) custom-call(bf16[4,2048,128]{2,1,0:T(8,128)(2,1)} %bitcast.16, bf16[4,2048,128]{2,1,0:T(8,128)(2,1)} %bitcast.17, bf16[27,16,128]{2,1,0:T(8,128)(2,1)} %bitcast.19, bf16[16,16,16,32]{3,2,1,0:T(8,128)(2,1)} %bitcast.18), custom_call_target="tpu_custom_call" | custom-call | flops 9059696640 | bytes 8388608 | tf_op jit(solution)/shard_map/pallas_call | solution.py:467
  78.5 1.6 %slice.6 = f32[27,16,128]{2,1,0:T(8,128)} slice(f32[39,16,128]{2,1,0:T(8,128)} %get-tuple-element.4), slice={[0:27], [0:16], [0:128]} | slice | bytes 442368 | tf_op jit(solution)/shard_map/slice | solution.py:516
  80.1 1.6 %slice.7 = f32[27,16,128]{2,1,0:T(8,128)} slice(f32[28,16,128]{2,1,0:T(8,128)} %get-tuple-element.5), slice={[0:27], [0:16], [0:128]} | slice | bytes 442368 | tf_op jit(solution)/shard_map/slice | solution.py:516

commit v2 on v1

--- a/solution.py
+++ b/solution.py
@@ -165,13 +165,13 @@
     return u + 9 * (u // 9)
 
 
-def kernel(dp, parts, scaling, sizes, acts, pre, w_ref, g_ref, coarse_out, fine_out, *scratch):
+def kernel(dp, parts, scaling, sizes, acts_far, pre_far, w_ref, g_ref, coarse_out, fine_out, *scratch):
     coarse, middle, outer = scratch[0], scratch[9], scratch[18]
     share = (dp, parts, scaling)
     coarse_sum = Reduction(*share, coarse_out, lambda u: u, coarse, scratch[1:9])
     middle_sum = Reduction(*share, fine_out, middle_place, middle, scratch[10:18])
     outer_sum = Reduction(*share, fine_out, outer_place, outer, scratch[19:27])
-    (wbuf, gbuf, halo, sends, recvs, w_full, mixing, g_send, g_turned, g_mixed, g_cells, g_rows, values, thin, frame, delta) = scratch[27:]
+    (wbuf, gbuf, halo, sends, recvs, w_full, mixing, g_send, g_turned, g_mixed, g_cells, g_rows, values, thin, frame, delta, acts, pre, loads) = scratch[27:]
     depth, across, height, channels = sizes
     half_x, half_y, half_z = depth // 2, across // 2, height // 2
     plane, small = across * height, half_y * half_z
@@ -182,6 +182,10 @@
     half = (w_ref.shape[0] + 1) // 2
     beside = me + 1 - 2 * lax.rem(me, 2)
     hello(dp, parts)
+    load_pre = pltpu.make_async_copy(pre_far, pre, loads.at[0])
+    load_acts = pltpu.make_async_copy(acts_far, acts, loads.at[1])
+    load_pre.start()
+    load_acts.start()
 
     count = 128 // half_y
 
@@ -226,7 +230,7 @@
         {"space": lax.rem(me + parts - 1, parts)},
     )
 
-    at_z = lax.broadcasted_iota(jnp.int32, (small, channels), 0) % half_z
+    at_z = lax.broadcasted_iota(jnp.int32, (half_y, half_z, channels), 1).reshape(small, channels)
 
     def spread(x, carry):
         values[x] = pre[x].astype(f32).reshape(half_y, 2, height, channels)
@@ -244,9 +248,11 @@
         thin[x, 1, 0:half_z, :] = jnp.zeros((half_z, 3 * channels), bf16)
         return carry
 
+    load_pre.wait()
     lax.fori_loop(0, depth, spread, 0)
 
-    at_cell = lax.broadcasted_iota(jnp.int32, (plane, channels), 0) % height
+    at_cell = lax.broadcasted_iota(jnp.int32, (across, height, channels), 1)
+    at_cell = at_cell.reshape(plane, channels)
 
     def place(q, cells):
         cells = cells.astype(f32)
@@ -264,6 +270,7 @@
         place(x + 1, acts[x])
         return carry
 
+    load_acts.wait()
     lax.fori_loop(0, depth, place_own, 0)
 
     def take_cotangents(s, block):
@@ -290,9 +297,6 @@
         copy = remote(block, block, sends.at[3, i], recvs.at[3, i], {"dp": partner})
         copy.start()
         forwards.append((0, i, copy))
-    pl.when(me < parts - 1)(upward.start)
-    pl.when(me > 0)(downward.start)
-
     for tap_x in range(3):
         for tap_y in range(3):
             total = None
@@ -316,6 +320,8 @@
         copy = remote(block, block, sends.at[4, i], recvs.at[4, i], {"dp": partner})
         copy.start()
         forwards.append((1, i, copy))
+    pl.when(me < parts - 1)(upward.start)
+    pl.when(me > 0)(downward.start)
 
     for p in range(half_x + 1):
         cells = g_cells[p]
@@ -382,20 +388,16 @@
     def layer(q):
         low, high = max(0, q - 2), min(depth - 1, q)
 
-        def step(tap_y, carry):
-            rhs = frame[q, pl.ds(pl.multiple_of(tap_y * height, height), plane), :]
-            lhs = delta[low * channels : (high + 1) * channels, :]
-            total = jnp.dot(lhs, rhs, preferred_element_type=f32)
-            for x in range(low, high + 1):
-                into, first = (middle, 0) if q - x == 1 else (outer, 9 * ((q - x) // 2))
-                for tap_z in range(3):
-                    into[first + 3 * tap_y + tap_z] += total[
-                        (x - low) * channels : (x - low + 1) * channels,
-                        tap_z * channels : (tap_z + 1) * channels,
-                    ]
-            return carry
-
-        lax.fori_loop(0, 3, step, 0)
+        slabs = [frame[q, y * height : y * height + plane, :] for y in range(3)]
+        lhs = delta[low * channels : (high + 1) * channels, :]
+        total = jnp.dot(lhs, jnp.concatenate(slabs, axis=1), preferred_element_type=f32)
+        for x in range(low, high + 1):
+            into, first = (middle, 0) if q - x == 1 else (outer, 9 * ((q - x) // 2))
+            for tap in range(9):
+                into[first + tap] += total[
+                    (x - low) * channels : (x - low + 1) * channels,
+                    tap * channels : (tap + 1) * channels,
+                ]
 
     layer(1)
     coarse_sum.to_space()
@@ -469,7 +471,7 @@
         out_shape=[
             jax.ShapeDtypeStruct((n, rows, channels), f32) for n in (units[0], max(units[1:]))
         ],
-        in_specs=[pl.BlockSpec(memory_space=VMEM)] * 4,
+        in_specs=[pl.BlockSpec(memory_space=pl.ANY)] * 2 + [pl.BlockSpec(memory_space=VMEM)] * 2,
         out_specs=[pl.BlockSpec(memory_space=VMEM)] * 2,
         scratch_shapes=reduction_scratch(dp, parts, channels, 27)
         + reduction_scratch(dp, parts, channels, 9)
@@ -491,6 +493,9 @@
             VMEM((depth, 2, small + half_z, 3 * channels), bf16),
             VMEM((depth + 2, plane + 2 * height, 3 * channels), bf16),
             VMEM((depth * channels, plane), bf16),
+            VMEM((depth, plane, channels), bf16),
+            VMEM((depth, plane, channels), bf16),
+            pltpu.SemaphoreType.DMA((2,)),
         ],
         cost_estimate=pl.CostEstimate(flops=flops, bytes_accessed=8 << 20, transcendentals=0),
         compiler_params=pltpu.CompilerParams(

time: 81.9 us -> 79.4 us (0.969)
  Pallas kernels: 77.8 us -> 75.3 us
    pallas_call x1, Pallas kernels: 77.8 us -> 75.3 us  [gradients(): pl.pallas_call(functools.partial(kernel, dp, parts, scaling, sizes), out_...]
where the time goes in v2:
time: 79.4 us; the launch traced here: 79.2 us
  Pallas kernels  75.3 us (95%)
  local copies, waits for them, and re-layouts  3.27 us (4%)
    pallas_call x1, Pallas kernels, gradients(): pl.pallas_call(functools.partial(kernel, dp, parts, scaling, sizes), out_...  75.3 us
    slice x2, local copies, waits for them, and re-layouts, by_filter(): taps = totals[:27]  3.27 us

profile of v2, /device:TPU:0, one launch (start us, length us, event | category | flops | bytes accessed | tf_op | source)
XLA Modules:
  0.0 79.2 jit_solution(9274053220346361955)
XLA Ops:
  0.6 75.3 %shard_map.59 = (f32[28,16,128]{2,1,0:T(8,128)}, f32[39,16,128]{2,1,0:T(8,128)}) custom-call(bf16[4,2048,128]{2,1,0:T(8,128)(2,1)} %bitcast.16, bf16[4,2048,128]{2,1,0:T(8,128)(2,1)} %bitcast.17, bf16[27,16,128]{2,1,0:T(8,128)(2,1)} %bitcast.19, bf16[16,16,16,32]{3,2,1,0:T(8,128)(2,1)} %bitcast.18), custom_call_target="tpu_custom_call" | custom-call | flops 9059696640 | bytes 8388608 | tf_op jit(solution)/shard_map/pallas_call | solution.py:469
  76.0 1.6 %slice.6 = f32[27,16,128]{2,1,0:T(8,128)} slice(f32[39,16,128]{2,1,0:T(8,128)} %get-tuple-element.4), slice={[0:27], [0:16], [0:128]} | slice | bytes 442368 | tf_op jit(solution)/shard_map/slice | solution.py:521
  77.6 1.6 %slice.7 = f32[27,16,128]{2,1,0:T(8,128)} slice(f32[28,16,128]{2,1,0:T(8,128)} %get-tuple-element.5), slice={[0:27], [0:16], [0:128]} | slice | bytes 442368 | tf_op jit(solution)/shard_map/slice | solution.py:521

commit v3 on v2

--- a/solution.py
+++ b/solution.py
@@ -216,14 +216,14 @@
     copy.start()
     w_beside.append(copy)
     upward = remote(
-        acts.at[depth - 1],
+        acts_far.at[depth - 1],
         halo.at[0],
         sends.at[5, 0],
         recvs.at[5, 0],
         {"space": lax.rem(me + 1, parts)},
     )
     downward = remote(
-        acts.at[0],
+        acts_far.at[0],
         halo.at[1],
         sends.at[5, 1],
         recvs.at[5, 1],
@@ -281,6 +281,8 @@
     for d in range(1, parts):
         g_copies[d - 1].wait_recv()
         take_cotangents(lax.rem(me + parts - d, parts), gbuf[d - 1])
+    pl.when(me < parts - 1)(upward.start)
+    pl.when(me > 0)(downward.start)
     for p in range(half_x + 1):
         g_mixed[p] = g_turned[p].T
         for y in range(half_y):
@@ -320,9 +322,6 @@
         copy = remote(block, block, sends.at[4, i], recvs.at[4, i], {"dp": partner})
         copy.start()
         forwards.append((1, i, copy))
-    pl.when(me < parts - 1)(upward.start)
-    pl.when(me > 0)(downward.start)
-
     for p in range(half_x + 1):
         cells = g_cells[p]
         later = jnp.where(at_z == half_z - 1, 0.0, pltpu.roll(cells, small - 1, 0))
@@ -371,8 +370,8 @@
                     values[where] = piece.reshape(half_y, half_z, channels)
         for odd_x in (0, 1):
             x = 2 * p + odd_x
-            cells = values[x].reshape(plane, channels)
-            delta[pl.ds(pl.multiple_of(x * channels, channels), channels), :] = cells.T.astype(bf16)
+            cells = values[x].reshape(plane, channels).astype(bf16)
+            delta[pl.ds(pl.multiple_of(x * channels, channels), channels), :] = cells.T
         return carry
 
     lax.fori_loop(0, half_x, propagate, 0)

time: 79.4 us -> 86.9 us (1.094)
  Pallas kernels: 75.3 us -> 82.8 us
    pallas_call x1, Pallas kernels: 75.3 us -> 82.8 us  [gradients(): pl.pallas_call(functools.partial(kernel, dp, parts, scaling, sizes), out_...]
where the time goes in v3:
time: 86.9 us; the launch traced here: 86.7 us
  Pallas kernels  82.8 us (95%)
  local copies, waits for them, and re-layouts  3.27 us (4%)
    pallas_call x1, Pallas kernels, gradients(): pl.pallas_call(functools.partial(kernel, dp, parts, scaling, sizes), out_...  82.8 us
    slice x2, local copies, waits for them, and re-layouts, by_filter(): taps = totals[:27]  3.27 us

profile of v3, /device:TPU:0, one launch (start us, length us, event | category | flops | bytes accessed | tf_op | source)
XLA Modules:
  0.0 86.7 jit_solution(2502216164501848842)
XLA Ops:
  0.6 82.8 %shard_map.59 = (f32[28,16,128]{2,1,0:T(8,128)}, f32[39,16,128]{2,1,0:T(8,128)}) custom-call(bf16[4,2048,128]{2,1,0:T(8,128)(2,1)} %bitcast.16, bf16[4,2048,128]{2,1,0:T(8,128)(2,1)} %bitcast.17, bf16[27,16,128]{2,1,0:T(8,128)(2,1)} %bitcast.19, bf16[16,16,16,32]{3,2,1,0:T(8,128)(2,1)} %bitcast.18), custom_call_target="tpu_custom_call" | custom-call | flops 9059696640 | bytes 8388608 | tf_op jit(solution)/shard_map/pallas_call | solution.py:468
  83.4 1.6 %slice.6 = f32[27,16,128]{2,1,0:T(8,128)} slice(f32[39,16,128]{2,1,0:T(8,128)} %get-tuple-element.4), slice={[0:27], [0:16], [0:128]} | slice | bytes 442368 | tf_op jit(solution)/shard_map/slice | solution.py:520
  85.1 1.6 %slice.7 = f32[27,16,128]{2,1,0:T(8,128)} slice(f32[28,16,128]{2,1,0:T(8,128)} %get-tuple-element.5), slice={[0:27], [0:16], [0:128]} | slice | bytes 442368 | tf_op jit(solution)/shard_map/slice | solution.py:520
